TPU v7x, 32 devices: a whole 2x2x4 slice. The times are simulated.
32 devices in a mesh: term: 2 (over y), pass: 16 (over z, x, core).
Axes of the slice: x: 2, y: 2, z: 4, core: 2. Of those that a mesh axis runs over, the one named last changes fastest.
Arguments:
- hidden: bfloat16 [8192, 4096], P('pass', 'term'), may hold values from -16 to 16
- head_weight: bfloat16 [4096, 16384], P('pass', 'term'), may hold values from -0.09375 to 0.09375
- lengths: int32 [128], P('pass'), may hold values from 1 to 64, as said below
Outputs:
- postings: bfloat16 [16384, 128], P(('term', 'pass'))
Inputs may be any that keep to these rules, and one draw needn't show every extreme that they name: Passage p's valid tokens are its first lengths[p] slots; some passage has exactly 64.
All inputs are finite; a program needn't handle non-finite values.
Results may differ from a plain program's by a relative error of at most 0.013.
Values may be sent and summed in bfloat16 or wider, within the bound.
A program may use at most 128 MiB of HBM per device.

v0:
```python
import jax
import jax.numpy as jnp
from jax import lax
from jax.sharding import PartitionSpec as P


def body(hidden, head_weight, lengths):
    gathered = lax.all_gather(hidden, "term", axis=1, tiled=True)
    passages = lengths.shape[0]
    tokens_per = gathered.shape[0] // passages
    slab_cols = head_weight.shape[1]
    allowed = jnp.arange(tokens_per, dtype=jnp.int32)[None, :] < lengths[:, None]
    logits = jnp.dot(
        gathered,
        lax.all_gather(head_weight, "pass", axis=0, tiled=True),
        preferred_element_type=jnp.float32,
    )
    impacts = jnp.log1p(jnp.maximum(logits, jnp.float32(0.0)))
    impacts = impacts.reshape(passages, tokens_per, slab_cols)
    impacts = jnp.where(allowed[:, :, None], impacts, jnp.float32(0.0))
    pooled = jnp.max(impacts, axis=1).astype(jnp.bfloat16)
    owners = lax.axis_size("pass")
    range_cols = slab_cols // owners
    local_max = jnp.max(pooled.astype(jnp.float32), axis=0)
    column_max = lax.pmax(local_max, "pass")
    payload = (pooled.astype(jnp.float32) / (1.0 + column_max)[None, :]).astype(jnp.bfloat16)
    shaped = payload.reshape(passages, owners, range_cols)
    return jnp.transpose(
        lax.all_to_all(shaped, "pass", split_axis=1, concat_axis=0, tiled=True)[:, 0, :]
    )


def solution(mesh):
    return jax.shard_map(
        body,
        mesh=mesh,
        in_specs=(P("pass", "term"), P("pass", "term"), P("pass")),
        out_specs=P(("term", "pass"), None),
        check_vma=False,
    )
```

profile of v0, /device:TPU:0, one launch (start us, length us, event | category | flops | bytes accessed | tf_op | source)
XLA Modules:
  0.0 522.5 jit_solution(6854478526555661946)
XLA Ops:
  6.5 0.0 all-gather.3.cloned.1.call-start
  6.5 0.7 all-gather.3.cloned.1.call-update
  7.3 0.0 all-gather.5.cloned.1.call-start
  7.3 0.7 all-gather.5.cloned.1.call-update
  8.0 0.7 iota_compare_fusion
  8.7 59.6 %all-gather.3.cloned.1.call-done = bf16[512,4096]{1,0:T(8,128)(2,1)} async-done(((bf16[512,2048]{1,0:T(8,128)(2,1)}), bf16[512,4096]{1,0:T(8,128)(2,1)}) %all-gather.3.cloned.1.call-update) | async-done | bytes 4194320 | tf_op jit(solution)/shard_map/all_gather | solution.py:8
  68.4 327.7 %all-gather.5.cloned.1.call-done = bf16[4096,8192]{1,0:T(8,128)(2,1)} async-done(((bf16[256,8192]{1,0:T(8,128)(2,1)}), bf16[4096,8192]{1,0:T(8,128)(2,1)}) %all-gather.5.cloned.1.call-update) | async-done | bytes 67108880 | tf_op jit(solution)/shard_map/all_gather | solution.py:15
  396.1 47.2 %select_reduce_fusion = bf16[8,8192]{1,0:T(8,128)(2,1)S(1)} fusion(pred[8,64]{1,0:T(8,128)(4,1)S(1)} %iota_compare_fusion, bf16[512,4096]{1,0:T(8,128)(2,1)} %all-gather.3.cloned.1.call-done, bf16[4096,8192]{1,0:T(8,128)(2,1)} %all-gather.5.cloned.1.call-done), kind=kOutput, calls=%fused_computation | convolution fusion | flops 34376450048 | bytes 71434752 | tf_op jit(solution)/shard_map/dot_general | solution.py:13
  443.4 0.1 convert_reduce_fusion
  443.5 60.7 %pmax.7 = f32[8192]{0:T(1024)S(1)} all-reduce(bf16[8192]{0:T(1024)(128)(2,1)S(1)} %get-tuple-element.5), channel_id=1, replica_groups=mesh['term'=2,'pass'=16] {'pass'}, use_global_device_ids=true, to_apply=%region_2.3 | all-reduce | flops 8192 | bytes 49152 | tf_op jit(solution)/shard_map/pmax | solution.py:25
  504.2 0.2 fusion
  504.3 0.1 copy.6
  504.4 10.5 %all_to_all.15 = bf16[8,16,512]{2,0,1:T(8,128)(2,1)S(1)} all-to-all(bf16[8,16,512]{2,0,1:T(8,128)(2,1)S(1)} %copy.6), channel_id=1, replica_groups=mesh['term'=2,'pass'=16] {'pass'}, dimensions={1} | all-to-all | bytes 262144 | tf_op jit(solution)/shard_map/all_to_all | solution.py:29
  514.9 0.8 copy.7
  (2 shorter events, 0.0 us)
Async XLA Ops:
  6.5 61.8 %all-gather.3.cloned.1.call-start = ((), (), s32[]{:S(2)}) async-start(), calls=%async_computation.1 | async-start | bytes 6291456 | tf_op jit(solution)/shard_map/all_gather | solution.py:8
  7.3 388.9 %all-gather.5.cloned.1.call-start = ((), (), s32[]{:S(2)}) async-start(), calls=%async_computation.2 | async-start | bytes 71303168 | tf_op jit(solution)/shard_map/all_gather | solution.py:15
Sparse Core Ops, SparseCore 0:
  8.9 59.4 all-gather.2
  70.0 326.0 all-gather.4
where the time goes:
time: 523 us
  waiting for transfers between devices  389 us (74%)
  blocking collectives  71.2 us (14%)
  matrix products  47.2 us (9%)
  between operations  13.4 us (3%)
    all_gather x1, waiting for transfers between devices, body(): lax.all_gather(head_weight, 'pass', axis=0, tiled=True)  328 us
    pmax x1, blocking collectives, body(): column_max = lax.pmax(local_max, 'pass')  60.7 us
    all_gather x1, waiting for transfers between devices, body(): gathered = lax.all_gather(hidden, 'term', axis=1, tiled=True)  59.6 us
    dot_general x1, matrix products, body(): jnp.dot(gathered, lax.all_gather(head_weight, 'pass', axis=0, tiled=True)...  47.2 us
    all_to_all x1, blocking collectives, body(): lax.all_to_all(shaped, 'pass', split_axis=1, concat_axis=0, tiled=True)  10.5 us
  transfers between devices with their start and end apart: 2, of which 2 were waited for; matrix products, arithmetic and copies ran while one was open for 0% of the time, Pallas kernels for 0%

commit v1 on v0

v1 whole, which is shorter than its diff:
```python
import jax
import jax.numpy as jnp
from jax import lax
from jax.sharding import PartitionSpec as P


def body(hidden, head_weight, lengths):
    terms = lax.axis_size("term")
    owners = lax.axis_size("pass")
    passages = lengths.shape[0]
    tokens_per = hidden.shape[0] // passages
    slab_cols = head_weight.shape[1]
    range_cols = slab_cols // owners
    own = lax.all_to_all(hidden, "term", split_axis=0, concat_axis=1, tiled=True)
    tokens = lax.all_gather(own, "pass", axis=0, tiled=True)
    rows = lax.all_to_all(head_weight, "pass", split_axis=1, concat_axis=0, tiled=True)
    weights = lax.all_gather(rows, "term", axis=1, tiled=True)
    share = passages // terms
    every = lax.all_gather(lengths, "pass", axis=0, tiled=True).reshape(owners, terms, share)
    mine = lax.dynamic_index_in_dim(every, lax.axis_index("term"), 1, False).reshape(-1)
    logits = jnp.dot(tokens, weights, preferred_element_type=jnp.float32)
    logits = logits.reshape(owners * share, tokens_per, terms * range_cols)
    allowed = jnp.arange(tokens_per, dtype=jnp.int32)[None, :] < mine[:, None]
    top = jnp.max(jnp.where(allowed[:, :, None], logits, jnp.float32(0.0)), axis=1)
    pooled = jnp.log1p(jnp.maximum(top, jnp.float32(0.0))).astype(jnp.bfloat16)
    got = lax.all_to_all(
        pooled.reshape(owners * share, terms, range_cols), "term", split_axis=1, concat_axis=1, tiled=True
    )
    full = got.reshape(owners, share, terms, range_cols).transpose(0, 2, 1, 3)
    full = full.reshape(owners * passages, range_cols).astype(jnp.float32)
    peak = jnp.max(full, axis=0)
    return jnp.transpose((full / (1.0 + peak)[None, :]).astype(jnp.bfloat16))


def solution(mesh):
    return jax.shard_map(
        body,
        mesh=mesh,
        in_specs=(P("pass", "term"), P("pass", "term"), P("pass")),
        out_specs=P(("term", "pass"), None),
        check_vma=False,
    )
```

time: 523 us -> 475 us (0.908)
  waiting for transfers between devices: 389 us -> 190 us
  blocking collectives: 71.2 us -> 210 us
  local copies, waits for them, and re-layouts: 0.85 us -> 17.4 us
    all_gather x2, waiting for transfers between devices: 387 us -> 190 us  [the longest x1 178 us: body(): tokens = lax.all_gather(own, 'pass', axis=0, tiled=True)]
    all_to_all x1 -> x3, blocking collectives: 10.5 us -> 152 us  [the longest x1 99.7 us: body(): lax.all_to_all(head_weight, 'pass', split_axis=1, concat_axis=0, tiled=True)]
    pmax x1 -> x0, blocking collectives: 60.7 us -> none  [body(): column_max = lax.pmax(local_max, 'pass')]
    unnamed x0 -> x1, blocking collectives: none -> 58.5 us
    all_to_all x0 -> x2, local copies, waits for them, and re-layouts: none -> 8.92 us  [the longest x1 6.4 us: body(): lax.all_to_all(head_weight, 'pass', split_axis=1, concat_axis=0, tiled=True)]
    unnamed x0 -> x8, local copies, waits for them, and re-layouts: none -> 7.21 us
  transfers between devices with their start and end apart: 2 -> 2, of which waited for: 2 -> 2; matrix products, arithmetic and copies ran while one was open for 0% -> 1% of each run, Pallas kernels for 0% -> 0%
where the time goes in v1:
time: 475 us; the launch traced here: 474 us
  blocking collectives  210 us (44%)
  waiting for transfers between devices  190 us (40%)
  matrix products  42 us (9%)
  local copies, waits for them, and re-layouts  17.4 us (4%)
  between operations  14.2 us (3%)
    all_gather x1, waiting for transfers between devices, body(): tokens = lax.all_gather(own, 'pass', axis=0, tiled=True)  178 us
    all_to_all x1, blocking collectives, body(): lax.all_to_all(head_weight, 'pass', split_axis=1, concat_axis=0, tiled=True)  99.7 us
    unnamed x1, blocking collectives  58.5 us
    all_to_all x1, blocking collectives, body(): lax.all_to_all(hidden, 'term', split_axis=0, concat_axis=1, tiled=True)  45.1 us
    dot_general x1, matrix products, body(): logits = jnp.dot(tokens, weights, preferred_element_type=jnp.float32)  42 us
    all_gather x1, waiting for transfers between devices, body(): weights = lax.all_gather(rows, 'term', axis=1, tiled=True)  12 us
  transfers between devices with their start and end apart: 2, of which 2 were waited for; matrix products, arithmetic and copies ran while one was open for 1% of the time, Pallas kernels for 0%

profile of v1, /device:TPU:0, one launch (start us, length us, event | category | flops | bytes accessed | tf_op | source)
XLA Modules:
  0.0 473.9 jit_solution(17428167600617619753)
XLA Ops:
  6.5 6.4 %copy.18 = bf16[256,8192]{0,1:T(8,128)(2,1)} copy(bf16[256,8192]{1,0:T(8,128)(2,1)} %param.4) | data formatting | bytes 8388608 | tf_op args[1]
  12.9 99.7 %all_to_all.43 = bf16[256,16,512]{0,2,1:T(8,128)(2,1)} all-to-all(bf16[256,16,512]{0,2,1:T(8,128)(2,1)} %bitcast.22), channel_id=1, replica_groups=mesh['term'=2,'pass'=16] {'pass'}, dimensions={1} | all-to-all | bytes 8388608 | tf_op jit(solution)/shard_map/all_to_all | solution.py:16
  112.6 6.4 %copy.19 = bf16[16,256,512]{2,1,0:T(8,128)(2,1)} copy(bf16[16,256,512]{1,2,0:T(8,128)(2,1)} %bitcast.21) | data formatting | bytes 8388608 | tf_op jit(solution)/shard_map/all_to_all | solution.py:16
  119.0 0.0 all-gather.5.cloned.1.call-update
  119.1 0.0 all-gather.3.cloned.1.call-start
  119.1 45.1 %all_to_all.44 = bf16[2,256,2048]{2,1,0:T(8,128)(2,1)S(1)} all-to-all(bf16[2,256,2048]{2,1,0:T(8,128)(2,1)} %bitcast.25), channel_id=1, replica_groups=mesh['term'=2,'pass'=16] {'term'}, dimensions={0} | all-to-all | bytes 4194304 | tf_op jit(solution)/shard_map/all_to_all | solution.py:14
  164.2 2.5 copy.17
  166.7 0.0 all-gather.3.cloned.1.call-update
  166.7 0.0 copy-done.1
  166.7 0.6 dynamic-slice
  168.0 0.2 dynamic-update-slice
  168.2 0.1 reshape.53
  168.3 58.5 %all-reduce.1 = s32[16,2,4]{2,1,0:T(2,128)S(1)} all-reduce(s32[16,2,4]{2,1,0:T(2,128)S(1)} %reshape.53), channel_id=1, replica_groups=mesh['term'=2,'pass'=16] {'pass'}, use_global_device_ids=true, to_apply=%add | all-reduce | flops 128 | bytes 1024
  226.9 0.1 lt.25
  227.0 0.1 iota_compare_fusion
  227.0 12.0 %all-gather.5.cloned.1.call-done = bf16[4096,1024]{1,0:T(8,128)(2,1)} async-done(((bf16[4096,512]{1,0:T(8,128)(2,1)}), bf16[4096,1024]{1,0:T(8,128)(2,1)}) %all-gather.5.cloned.1.call-update) | async-done | bytes 8388624 | tf_op jit(solution)/shard_map/all_gather | solution.py:17
  239.0 177.7 %all-gather.3.cloned.1.call-done = bf16[4096,4096]{0,1:T(8,128)(2,1)} async-done(((bf16[256,4096]{0,1:T(8,128)(2,1)}), bf16[4096,4096]{0,1:T(8,128)(2,1)}) %all-gather.3.cloned.1.call-update) | async-done | bytes 33554448 | tf_op jit(solution)/shard_map/all_gather | solution.py:15
  416.8 42.0 %select_reduce_fusion = f32[64,1024]{1,0:T(8,128)S(1)} fusion(pred[64,64]{1,0:T(8,128)(4,1)S(1)} %iota_compare_fusion, bf16[4096,4096]{0,1:T(8,128)(2,1)} %all-gather.3.cloned.1.call-done, bf16[4096,1024]{1,0:T(8,128)(2,1)} %all-gather.5.cloned.1.call-done), kind=kOutput, calls=%fused_computation | convolution fusion | flops 34368061440 | bytes 42209280 | tf_op jit(solution)/shard_map/dot_general | solution.py:21
  458.8 0.1 log-plus-one_convert_fusion
  458.9 7.0 %all_to_all.45 = bf16[64,2,512]{2,0,1:T(8,128)(2,1)S(1)} all-to-all(bf16[64,2,512]{2,0,1:T(8,128)(2,1)S(1)} %bitcast.28), channel_id=1, replica_groups=mesh['term'=2,'pass'=16] {'term'}, dimensions={1} | all-to-all | bytes 262144 | tf_op jit(solution)/shard_map/all_to_all | solution.py:26
  465.9 0.1 copy.21
  466.1 0.1 copy.22
  466.2 0.1 reshape.55
  466.3 0.8 copy.23
  (10 shorter events, 0.1 us)
Async XLA Ops:
  6.5 232.5 %all-gather.5.cloned.1.call-start = ((), (), s32[]{:S(2)}) async-start(), calls=%async_computation.4 | async-start | bytes 12582912 | tf_op jit(solution)/shard_map/all_gather | solution.py:17
  119.0 47.7 %copy-start.1 = (u32[32]{0:T(128)S(1)}, u32[32]{0:T(128)}, u32[]{:S(2)}) copy-start(u32[32]{0:T(128)} %constant.24) | copy-start | bytes 388
  119.0 48.9 %copy-start = (s32[8]{0:T(128)S(1)}, s32[8]{0:T(128)}, u32[]{:S(2)}) copy-start(s32[8]{0:T(128)} %param.5) | copy-start | bytes 100
  119.1 297.7 %all-gather.3.cloned.1.call-start = ((), (), s32[]{:S(2)}) async-start(), calls=%async_computation.3 | async-start | bytes 35651584 | tf_op jit(solution)/shard_map/all_gather | solution.py:15
Sparse Core Ops, SparseCore 0:
  119.2 119.8 all-gather.4
  240.6 176.1 all-gather.2

commit v2 on v1

v2 whole, which is shorter than its diff:
```python
import functools

import jax
import jax.numpy as jnp
from jax import lax
from jax.experimental import pallas as pl
from jax.experimental.pallas import tpu as pltpu
from jax.sharding import PartitionSpec as P

MESH = pl.DeviceIdType.MESH
ZS, XS, CS = 4, 2, 2
CHUNKS = 4
HIGHEST_VMEM = 58 * 1024 * 1024


def kernel(
    tokens_per, hid, head, out,
    tok, wts, pool, give, take,
    s_up, s_dn, r_z, s_y, r_y, s_c, r_c, s_h, r_h, s_x, r_x, s_f, r_f, s_l,
):
    y = lax.axis_index("term")
    me = lax.axis_index("pass")
    z, x, c = me // (XS * CS), (me // CS) % XS, me % CS
    block, feats = hid.shape
    feat_rows = head.shape[0]
    cols = wts.shape[2]
    rows = block // CHUNKS
    per = block // tokens_per

    def at(zz, xx, cc):
        return (zz * XS + xx) * CS + cc

    y_dev = (1 - y, me)
    x_dev = (y, at(z, 1 - x, c))
    c_dev = (y, at(z, x, 1 - c))
    up_dev = (y, at(jnp.minimum(z + 1, ZS - 1), x, c))
    dn_dev = (y, at(jnp.maximum(z - 1, 0), x, c))

    def others(do):
        for i in range(1, ZS):
            zz = lax.rem(z + i, ZS)
            for cc in range(CS):
                do(zz, cc)
        do(z, 1 - c)

    barrier = pltpu.get_barrier_semaphore()

    def hello(dev):
        pl.semaphore_signal(barrier, inc=1, device_id=dev, device_id_type=MESH)

    others(lambda zz, cc: hello((y, at(zz, x, cc))))
    hello(x_dev)
    hello(y_dev)
    pl.semaphore_wait(barrier, ZS * CS + 1)

    def remote(src, dst, send, recv, dev):
        return pltpu.make_async_remote_copy(
            src_ref=src, dst_ref=dst, send_sem=send, recv_sem=recv,
            device_id=dev, device_id_type=MESH,
        )

    def piece(f, zz, cc, k):
        return tok.at[f, zz, cc, pl.ds(k * rows, rows)]

    def own_piece(k):
        return hid.at[pl.ds(k * rows, rows)]

    def up(zz, k, src):
        return remote(src, piece(y, zz, c, k), s_up.at[zz, k], r_z.at[zz, k], up_dev)

    def down(zz, k, src):
        return remote(src, piece(y, zz, c, k), s_dn.at[zz, k], r_z.at[zz, k], dn_dev)

    def across_y(zz, k, src):
        return remote(src, piece(y, zz, c, k), s_y.at[zz, k], r_y.at[zz, k], y_dev)

    def across_c(f, zz, k, src):
        return remote(src, piece(f, zz, c, k), s_c.at[f, zz, k], r_c.at[f, zz, k], c_dev)

    def strip(zz, cc, xx):
        first = at(zz, xx, cc) * cols
        return head.at[:, pl.ds(pl.multiple_of(first, cols), cols)]

    def wts_of(p, xx):
        return wts.at[xx, pl.ds(pl.multiple_of(p * feat_rows, feat_rows), feat_rows)]

    def both_of(p):
        return wts.at[:, pl.ds(pl.multiple_of(p * feat_rows, feat_rows), feat_rows)]

    def head_to(zz, cc, xx):
        return remote(
            strip(zz, cc, xx), wts_of(me, xx),
            s_h.at[zz * CS + cc, xx], r_h.at[z * CS + c, xx], (y, at(zz, x, cc)),
        )

    def head_from(zz, cc, xx):
        ref = wts_of(at(zz, x, cc), xx)
        return remote(ref, ref, s_h.at[zz * CS + cc, xx], r_h.at[zz * CS + cc, xx], x_dev)

    def relay(zz, cc):
        ref = both_of(at(zz, x, cc))
        return remote(ref, ref, s_x.at[zz * CS + cc], r_x.at[zz * CS + cc], x_dev)

    def send_head(zz, cc):
        for xx in range(XS):
            head_to(zz, cc, xx).start()

    others(send_head)
    local = [pltpu.make_async_copy(strip(z, c, xx), wts_of(me, xx), s_l.at[xx]) for xx in range(XS)]
    local.append(pltpu.make_async_copy(hid, tok.at[y, z, c], s_l.at[XS]))
    for copy in local:
        copy.start()
    for k in range(CHUNKS):
        @pl.when(z < ZS - 1)
        def _():
            up(z, k, own_piece(k)).start()

        @pl.when(z > 0)
        def _():
            down(z, k, own_piece(k)).start()

        across_y(z, k, own_piece(k)).start()
        across_c(y, z, k, own_piece(k)).start()
    for copy in local:
        copy.wait()
    relay(z, c).start()

    def pass_head(zz, cc):
        for xx in range(XS):
            head_from(zz, cc, xx).wait_recv()
        relay(zz, cc).start()

    others(pass_head)

    def multiply(zz, cc):
        def half(xx, carry):
            acc = jnp.dot(tok[0, zz, cc], wts[xx, pl.ds(0, feats)], preferred_element_type=jnp.float32)
            acc += jnp.dot(tok[1, zz, cc], wts[xx, pl.ds(feats, feats)], preferred_element_type=jnp.float32)
            top = jnp.max(acc.reshape(per, tokens_per, cols), axis=1)
            first = pl.multiple_of((zz * CS + cc) * per, per)
            pool[xx, pl.ds(first, per), :] = jnp.log1p(jnp.maximum(top, 0.0))
            return carry

        lax.fori_loop(0, XS, half, 0)

    def step(d, carry):
        for k in range(CHUNKS):
            below, above = z - d - 1, z + d + 1

            @pl.when(below >= 0)
            def _():
                src = piece(y, below, c, k)
                up(below, k, src).wait_recv()

                @pl.when(z < ZS - 1)
                def _():
                    up(below, k, src).start()

                across_y(below, k, src).start()
                across_c(y, below, k, src).start()

            @pl.when(above < ZS)
            def _():
                src = piece(y, above, c, k)
                down(above, k, src).wait_recv()

                @pl.when(z > 0)
                def _():
                    down(above, k, src).start()

                across_y(above, k, src).start()
                across_c(y, above, k, src).start()

        def sides(do):
            def side(s, inner):
                zz = z + (1 - 2 * s) * d

                @pl.when((zz >= 0) & (zz < ZS) & ((d > 0) | (s == 0)))
                def _():
                    do(zz)

                return inner

            lax.fori_loop(0, 2, side, 0)

        def from_y(zz):
            for k in range(CHUNKS):
                src = piece(1 - y, zz, c, k)
                across_y(zz, k, src).wait_recv()
                across_c(1 - y, zz, k, src).start()

        sides(from_y)

        @pl.when(d == 0)
        def _():
            for i in range(ZS * CS):
                relay(i // CS, i % CS).wait_recv()

        def use(zz):
            def core(i, inner):
                cc = lax.rem(c + i, CS)

                @pl.when(i == 1)
                def _():
                    for f in range(2):
                        for k in range(CHUNKS):
                            across_c(f, zz, k, piece(f, zz, c, k)).wait_recv()

                multiply(zz, cc)
                return inner

            lax.fori_loop(0, CS, core, 0)

        sides(use)
        return carry

    lax.fori_loop(0, ZS, step, 0)

    give[...] = pool[1 - x].astype(jnp.bfloat16)
    last = remote(give, take, s_f, r_f, x_dev)
    last.start()

    def sent(zz, carry):
        for k in range(CHUNKS):
            @pl.when((zz <= z) & (z < ZS - 1))
            def _():
                up(zz, k, own_piece(k)).wait_send()

            @pl.when((zz >= z) & (z > 0))
            def _():
                down(zz, k, own_piece(k)).wait_send()

            across_y(zz, k, own_piece(k)).wait_send()
            for f in range(2):
                across_c(f, zz, k, own_piece(k)).wait_send()
        for cc in range(CS):
            relay(zz, cc).wait_send()
        return carry

    lax.fori_loop(0, ZS, sent, 0)

    def head_sent(zz, cc):
        for xx in range(XS):
            head_to(zz, cc, xx).wait_send()

    others(head_sent)
    last.wait()

    mine = pool[x].astype(jnp.bfloat16).astype(jnp.float32)
    theirs = take[...].astype(jnp.float32)
    even = jnp.where(x == 0, mine, theirs)
    odd = jnp.where(x == 0, theirs, mine)
    span = CS * per
    parts = []
    for zz in range(ZS):
        parts += [even[zz * span:(zz + 1) * span], odd[zz * span:(zz + 1) * span]]
    full = jnp.concatenate(parts, axis=0)
    peak = jnp.max(full, axis=0, keepdims=True)
    out[...] = jnp.transpose(full / (1.0 + peak)).astype(jnp.bfloat16)


def masked(hidden, lengths):
    passages = lengths.shape[0]
    tokens_per = hidden.shape[0] // passages
    allowed = jnp.arange(tokens_per, dtype=jnp.int32)[None, :] < lengths[:, None]
    return jnp.where(allowed.reshape(-1)[:, None], hidden, jnp.bfloat16(0.0))


def fused(hidden, head_weight, lengths):
    passages = lengths.shape[0]
    tokens = hidden.shape[0]
    feats = hidden.shape[1]
    feat_rows = head_weight.shape[0]
    cols = head_weight.shape[1] // (ZS * XS * CS)
    rows = ZS * CS * passages
    dma = pltpu.SemaphoreType.DMA
    return pl.pallas_call(
        functools.partial(kernel, tokens // passages),
        out_shape=jax.ShapeDtypeStruct((cols, XS * rows), jnp.bfloat16),
        in_specs=[pl.BlockSpec(memory_space=pl.ANY)] * 2,
        out_specs=pl.BlockSpec(memory_space=pltpu.VMEM),
        scratch_shapes=[
            pltpu.VMEM((2, ZS, CS, tokens, feats), jnp.bfloat16),
            pltpu.VMEM((XS, 2 * feats, cols), jnp.bfloat16),
            pltpu.VMEM((XS, rows, cols), jnp.float32),
            pltpu.VMEM((rows, cols), jnp.bfloat16),
            pltpu.VMEM((rows, cols), jnp.bfloat16),
            dma((ZS, CHUNKS)), dma((ZS, CHUNKS)), dma((ZS, CHUNKS)),
            dma((ZS, CHUNKS)), dma((ZS, CHUNKS)),
            dma((2, ZS, CHUNKS)), dma((2, ZS, CHUNKS)),
            dma((ZS * CS, XS)), dma((ZS * CS, XS)),
            dma((ZS * CS,)), dma((ZS * CS,)),
            dma, dma, dma((XS + 1,)),
        ],
        compiler_params=pltpu.CompilerParams(
            collective_id=0, has_side_effects=True, vmem_limit_bytes=HIGHEST_VMEM
        ),
        cost_estimate=pl.CostEstimate(
            flops=2 * ZS * CS * tokens * 2 * feats * XS * cols,
            bytes_accessed=2 * (tokens * feats + feat_rows * head_weight.shape[1]),
            transcendentals=0,
        ),
    )(masked(hidden, lengths), head_weight)


def general(hidden, head_weight, lengths):
    terms = lax.axis_size("term")
    owners = lax.axis_size("pass")
    passages = lengths.shape[0]
    tokens_per = hidden.shape[0] // passages
    range_cols = head_weight.shape[1] // owners
    own = lax.all_to_all(masked(hidden, lengths), "term", split_axis=0, concat_axis=1, tiled=True)
    tokens = lax.all_gather(own, "pass", axis=0, tiled=True)
    rows = lax.all_to_all(head_weight, "pass", split_axis=1, concat_axis=0, tiled=True)
    weights = lax.all_gather(rows, "term", axis=1, tiled=True)
    share = passages // terms
    logits = jnp.dot(tokens, weights, preferred_element_type=jnp.float32)
    logits = logits.reshape(owners * share, tokens_per, terms * range_cols)
    top = jnp.maximum(jnp.max(logits, axis=1), jnp.float32(0.0))
    pooled = jnp.log1p(top).astype(jnp.bfloat16)
    got = lax.all_to_all(
        pooled.reshape(owners * share, terms, range_cols), "term", split_axis=1, concat_axis=1, tiled=True
    )
    full = got.reshape(owners, share, terms, range_cols).transpose(0, 2, 1, 3)
    full = full.reshape(owners * passages, range_cols).astype(jnp.float32)
    peak = jnp.max(full, axis=0)
    return jnp.transpose((full / (1.0 + peak)[None, :]).astype(jnp.bfloat16))


def solution(mesh):
    small = mesh.shape["term"] == 2 and mesh.shape["pass"] == ZS * XS * CS
    return jax.shard_map(
        fused if small else general,
        mesh=mesh,
        in_specs=(P("pass", "term"), P("pass", "term"), P("pass")),
        out_specs=P(("term", "pass"), None),
        check_vma=False,
    )
```

time: 475 us -> 264 us (0.56)
  the two profiles are of different devices: /device:TPU:0 before, /device:TPU:16 now
where the time goes in v2:
time: 264 us
  Pallas kernels  258 us (98%)
  other arithmetic  3.88 us (1%)
    pallas_call x1, Pallas kernels, fused(): pl.pallas_call(functools.partial(kernel, tokens // passages), out_shape=j...  258 us

profile of v2, /device:TPU:16, one launch (start us, length us, event | category | flops | bytes accessed | tf_op | source)
XLA Modules:
  0.0 263.8 jit_solution(2936046807895623950)
XLA Ops:
  0.0 0.7 iota_compare_fusion
  0.7 0.1 lt.23
  0.8 3.2 %broadcast_select_fusion.hid = bf16[512,2048]{1,0:T(8,128)(2,1)} fusion(bf16[512,2048]{1,0:T(8,128)(2,1)} %param.3, pred[512]{0:T(512)(128)(4,1)S(1)} %lt.23), kind=kLoop, calls=%fused_computation | loop fusion | flops 1048576 | bytes 4194816 | tf_op jit(solution)/shard_map/jit(_where)/select_n | solution.py:266
  4.0 258.3 %shard_map.37 = bf16[512,128]{1,0:T(8,128)(2,1)} custom-call(bf16[512,2048]{1,0:T(8,128)(2,1)} %broadcast_select_fusion.hid, bf16[256,8192]{1,0:T(8,128)(2,1)} %head.1), custom_call_target="tpu_custom_call" | custom-call | flops 34359738368 | bytes 6291456 | tf_op jit(solution)/shard_map/pallas_call | solution.py:277
  262.3 1.6 copy.5

commit v3 on v2

--- a/solution.py
+++ b/solution.py
@@ -10,6 +10,7 @@
 MESH = pl.DeviceIdType.MESH
 ZS, XS, CS = 4, 2, 2
 CHUNKS = 4
+STEPS = 4
 HIGHEST_VMEM = 58 * 1024 * 1024
 
 
@@ -84,9 +85,6 @@
     def wts_of(p, xx):
         return wts.at[xx, pl.ds(pl.multiple_of(p * feat_rows, feat_rows), feat_rows)]
 
-    def both_of(p):
-        return wts.at[:, pl.ds(pl.multiple_of(p * feat_rows, feat_rows), feat_rows)]
-
     def head_to(zz, cc, xx):
         return remote(
             strip(zz, cc, xx), wts_of(me, xx),
@@ -97,124 +95,176 @@
         ref = wts_of(at(zz, x, cc), xx)
         return remote(ref, ref, s_h.at[zz * CS + cc, xx], r_h.at[zz * CS + cc, xx], x_dev)
 
-    def relay(zz, cc):
-        ref = both_of(at(zz, x, cc))
-        return remote(ref, ref, s_x.at[zz * CS + cc], r_x.at[zz * CS + cc], x_dev)
-
-    def send_head(zz, cc):
-        for xx in range(XS):
-            head_to(zz, cc, xx).start()
-
-    others(send_head)
+    def relay(zz, cc, xx):
+        ref = wts_of(at(zz, x, cc), xx)
+        return remote(ref, ref, s_x.at[zz * CS + cc, xx], r_x.at[zz * CS + cc, xx], x_dev)
+
+    def relay_from(zz, cc, xx):
+        ref = wts_of(at(zz, 1 - x, cc), xx)
+        return remote(ref, ref, s_x.at[zz * CS + cc, xx], r_x.at[zz * CS + cc, xx], x_dev)
+
+    def send_head(xx):
+        others(lambda zz, cc: head_to(zz, cc, xx).start())
+        relay(z, c, xx).start()
+
+    def pass_head(zz, cc, xx):
+        head_from(zz, cc, xx).wait_recv()
+        relay(zz, cc, xx).start()
+
+    def sides(d, do):
+        def side(s, inner):
+            zz = z + (1 - 2 * s) * d
+
+            @pl.when((zz >= 0) & (zz < ZS))
+            def _():
+                do(zz)
+
+            return inner
+
+        lax.fori_loop(0, 2, side, 0)
+
+    def pass_tokens(d, k):
+        below, above = z - d, z + d
+
+        @pl.when(below >= 0)
+        def _():
+            src = piece(y, below, c, k)
+            up(below, k, src).wait_recv()
+
+            @pl.when(z < ZS - 1)
+            def _():
+                up(below, k, src).start()
+
+            across_y(below, k, src).start()
+            across_c(y, below, k, src).start()
+
+        @pl.when(above < ZS)
+        def _():
+            src = piece(y, above, c, k)
+            down(above, k, src).wait_recv()
+
+            @pl.when(z > 0)
+            def _():
+                down(above, k, src).start()
+
+            across_y(above, k, src).start()
+            across_c(y, above, k, src).start()
+
+    def from_y(zz):
+        def one(k, carry):
+            src = piece(1 - y, zz, c, k)
+            across_y(zz, k, src).wait_recv()
+            across_c(1 - y, zz, k, src).start()
+            return carry
+
+        lax.fori_loop(0, CHUNKS, one, 0)
+
+    def pass_far_head(d):
+        def both(zz):
+            for cc in range(CS):
+                pass_head(zz, cc, 1)
+
+        sides(d, both)
+
+    def send_own(k, carry):
+        @pl.when(z < ZS - 1)
+        def _():
+            up(z, k, own_piece(k)).start()
+
+        @pl.when(z > 0)
+        def _():
+            down(z, k, own_piece(k)).start()
+
+        across_y(z, k, own_piece(k)).start()
+        across_c(y, z, k, own_piece(k)).start()
+        return carry
+
+    lax.fori_loop(0, CHUNKS, send_own, 0)
     local = [pltpu.make_async_copy(strip(z, c, xx), wts_of(me, xx), s_l.at[xx]) for xx in range(XS)]
     local.append(pltpu.make_async_copy(hid, tok.at[y, z, c], s_l.at[XS]))
     for copy in local:
         copy.start()
-    for k in range(CHUNKS):
-        @pl.when(z < ZS - 1)
-        def _():
-            up(z, k, own_piece(k)).start()
-
-        @pl.when(z > 0)
-        def _():
-            down(z, k, own_piece(k)).start()
-
-        across_y(z, k, own_piece(k)).start()
-        across_c(y, z, k, own_piece(k)).start()
     for copy in local:
         copy.wait()
-    relay(z, c).start()
-
-    def pass_head(zz, cc):
-        for xx in range(XS):
-            head_from(zz, cc, xx).wait_recv()
-        relay(zz, cc).start()
-
-    others(pass_head)
-
-    def multiply(zz, cc):
-        def half(xx, carry):
-            acc = jnp.dot(tok[0, zz, cc], wts[xx, pl.ds(0, feats)], preferred_element_type=jnp.float32)
-            acc += jnp.dot(tok[1, zz, cc], wts[xx, pl.ds(feats, feats)], preferred_element_type=jnp.float32)
-            top = jnp.max(acc.reshape(per, tokens_per, cols), axis=1)
-            first = pl.multiple_of((zz * CS + cc) * per, per)
-            pool[xx, pl.ds(first, per), :] = jnp.log1p(jnp.maximum(top, 0.0))
-            return carry
-
-        lax.fori_loop(0, XS, half, 0)
-
-    def step(d, carry):
-        for k in range(CHUNKS):
-            below, above = z - d - 1, z + d + 1
-
-            @pl.when(below >= 0)
-            def _():
-                src = piece(y, below, c, k)
-                up(below, k, src).wait_recv()
-
-                @pl.when(z < ZS - 1)
-                def _():
-                    up(below, k, src).start()
-
-                across_y(below, k, src).start()
-                across_c(y, below, k, src).start()
-
-            @pl.when(above < ZS)
-            def _():
-                src = piece(y, above, c, k)
-                down(above, k, src).wait_recv()
-
-                @pl.when(z > 0)
-                def _():
-                    down(above, k, src).start()
-
-                across_y(above, k, src).start()
-                across_c(y, above, k, src).start()
-
-        def sides(do):
-            def side(s, inner):
-                zz = z + (1 - 2 * s) * d
-
-                @pl.when((zz >= 0) & (zz < ZS) & ((d > 0) | (s == 0)))
-                def _():
-                    do(zz)
-
+
+    def first(k, carry):
+        @pl.when(k == CHUNKS // 2)
+        def _():
+            send_head(0)
+
+        pass_tokens(1, k)
+        return carry
+
+    def second(k, carry):
+        pass_tokens(2, k)
+        return carry
+
+    lax.fori_loop(0, CHUNKS, first, 0)
+    from_y(z)
+    lax.fori_loop(0, CHUNKS, second, 0)
+    send_head(1)
+    others(lambda zz, cc: pass_head(zz, cc, 0))
+    pass_head(z, 1 - c, 1)
+    sides(1, from_y)
+
+    def arrived(zz):
+        for f in range(2):
+            for k in range(CHUNKS):
+                across_c(f, zz, k, piece(f, zz, 1 - c, k)).wait_recv()
+
+    def multiply(zz, cc, xx):
+        acc = jnp.dot(tok[0, zz, cc], wts[xx, pl.ds(0, feats)], preferred_element_type=jnp.float32)
+        acc += jnp.dot(tok[1, zz, cc], wts[xx, pl.ds(feats, feats)], preferred_element_type=jnp.float32)
+        top = jnp.max(acc.reshape(per, tokens_per, cols), axis=1)
+        start = pl.multiple_of((zz * CS + cc) * per, per)
+        pool[xx, pl.ds(start, per), :] = jnp.log1p(jnp.maximum(top, 0.0))
+
+    def step(j, carry):
+        @pl.when(j < STEPS)
+        def _():
+            for i in range(CHUNKS // STEPS):
+                pass_tokens(3, j * (CHUNKS // STEPS) + i)
+
+        @pl.when(j == 0)
+        def _():
+            for i in range(ZS * CS):
+                relay_from(i // CS, i % CS, 0).wait_recv()
+
+        @pl.when(j == STEPS - 1)
+        def _():
+            pass_far_head(1)
+            sides(2, from_y)
+
+        @pl.when(j == STEPS + 1)
+        def _():
+            pass_far_head(2)
+            sides(3, from_y)
+            pass_far_head(3)
+
+        d, s = (j + 1) // 2, (j + 1) % 2
+        zz = z + (1 - 2 * s) * d
+
+        @pl.when((zz >= 0) & (zz < ZS))
+        def _():
+            arrived(zz)
+
+            def core(cc, inner):
+                multiply(zz, cc, 0)
                 return inner
 
-            lax.fori_loop(0, 2, side, 0)
-
-        def from_y(zz):
-            for k in range(CHUNKS):
-                src = piece(1 - y, zz, c, k)
-                across_y(zz, k, src).wait_recv()
-                across_c(1 - y, zz, k, src).start()
-
-        sides(from_y)
-
-        @pl.when(d == 0)
-        def _():
-            for i in range(ZS * CS):
-                relay(i // CS, i % CS).wait_recv()
-
-        def use(zz):
-            def core(i, inner):
-                cc = lax.rem(c + i, CS)
-
-                @pl.when(i == 1)
-                def _():
-                    for f in range(2):
-                        for k in range(CHUNKS):
-                            across_c(f, zz, k, piece(f, zz, c, k)).wait_recv()
-
-                multiply(zz, cc)
-                return inner
-
             lax.fori_loop(0, CS, core, 0)
 
-        sides(use)
-        return carry
-
-    lax.fori_loop(0, ZS, step, 0)
+        return carry
+
+    lax.fori_loop(0, 2 * ZS - 1, step, 0)
+    for i in range(ZS * CS):
+        relay_from(i // CS, i % CS, 1).wait_recv()
+
+    def rest(i, carry):
+        multiply(i // CS, i % CS, 1)
+        return carry
+
+    lax.fori_loop(0, ZS * CS, rest, 0)
 
     give[...] = pool[1 - x].astype(jnp.bfloat16)
     last = remote(give, take, s_f, r_f, x_dev)
@@ -234,7 +284,8 @@
             for f in range(2):
                 across_c(f, zz, k, own_piece(k)).wait_send()
         for cc in range(CS):
-            relay(zz, cc).wait_send()
+            for xx in range(XS):
+                relay(zz, cc, xx).wait_send()
         return carry
 
     lax.fori_loop(0, ZS, sent, 0)
@@ -289,7 +340,7 @@
             dma((ZS, CHUNKS)), dma((ZS, CHUNKS)),
             dma((2, ZS, CHUNKS)), dma((2, ZS, CHUNKS)),
             dma((ZS * CS, XS)), dma((ZS * CS, XS)),
-            dma((ZS * CS,)), dma((ZS * CS,)),
+            dma((ZS * CS, XS)), dma((ZS * CS, XS)),
             dma, dma, dma((XS + 1,)),
         ],
         compiler_params=pltpu.CompilerParams(

time: 264 us -> 288 us (1.091)
  the two profiles are of different devices: /device:TPU:16 before, /device:TPU:8 now
where the time goes in v3:
time: 288 us; the launch traced here: 287 us
  Pallas kernels  282 us (98%)
  other arithmetic  3.88 us (1%)
    pallas_call x1, Pallas kernels, fused(): pl.pallas_call(functools.partial(kernel, tokens // passages), out_shape=j...  282 us

profile of v3, /device:TPU:8, one launch (start us, length us, event | category | flops | bytes accessed | tf_op | source)
XLA Modules:
  0.0 287.4 jit_solution(6885946621854199761)
XLA Ops:
  0.0 0.7 iota_compare_fusion
  0.7 0.1 lt.23
  0.8 3.2 %broadcast_select_fusion.hid = bf16[512,2048]{1,0:T(8,128)(2,1)} fusion(bf16[512,2048]{1,0:T(8,128)(2,1)} %param.3, pred[512]{0:T(512)(128)(4,1)S(1)} %lt.23), kind=kLoop, calls=%fused_computation | loop fusion | flops 1048576 | bytes 4194816 | tf_op jit(solution)/shard_map/jit(_where)/select_n | solution.py:317
  4.0 281.9 %shard_map.37 = bf16[512,128]{1,0:T(8,128)(2,1)} custom-call(bf16[512,2048]{1,0:T(8,128)(2,1)} %broadcast_select_fusion.hid, bf16[256,8192]{1,0:T(8,128)(2,1)} %head.1), custom_call_target="tpu_custom_call" | custom-call | flops 34359738368 | bytes 6291456 | tf_op jit(solution)/shard_map/pallas_call | solution.py:328
  285.8 1.6 copy.5

commit v4 on v3

--- a/solution.py
+++ b/solution.py
@@ -1,5 +1,3 @@
-import functools
-
 import jax
 import jax.numpy as jnp
 from jax import lax
@@ -10,23 +8,19 @@
 MESH = pl.DeviceIdType.MESH
 ZS, XS, CS = 4, 2, 2
 CHUNKS = 4
-STEPS = 4
-HIGHEST_VMEM = 58 * 1024 * 1024
 
 
 def kernel(
-    tokens_per, hid, head, out,
-    tok, wts, pool, give, take,
-    s_up, s_dn, r_z, s_y, r_y, s_c, r_c, s_h, r_h, s_x, r_x, s_f, r_f, s_l,
+    hid, head, tok, wts,
+    s_up, s_dn, r_z, s_y, r_y, s_c, r_c, s_h, r_h, s_x, r_x, s_l,
 ):
     y = lax.axis_index("term")
     me = lax.axis_index("pass")
     z, x, c = me // (XS * CS), (me // CS) % XS, me % CS
     block, feats = hid.shape
     feat_rows = head.shape[0]
-    cols = wts.shape[2]
+    cols = wts.shape[1] // XS
     rows = block // CHUNKS
-    per = block // tokens_per
 
     def at(zz, xx, cc):
         return (zz * XS + xx) * CS + cc
@@ -61,7 +55,8 @@
         )
 
     def piece(f, zz, cc, k):
-        return tok.at[f, zz, cc, pl.ds(k * rows, rows)]
+        first = (zz * CS + cc) * block + k * rows
+        return tok.at[pl.ds(pl.multiple_of(first, rows), rows), pl.ds(pl.multiple_of(f * feats, feats), feats)]
 
     def own_piece(k):
         return hid.at[pl.ds(k * rows, rows)]
@@ -83,7 +78,7 @@
         return head.at[:, pl.ds(pl.multiple_of(first, cols), cols)]
 
     def wts_of(p, xx):
-        return wts.at[xx, pl.ds(pl.multiple_of(p * feat_rows, feat_rows), feat_rows)]
+        return wts.at[pl.ds(pl.multiple_of(p * feat_rows, feat_rows), feat_rows), pl.ds(xx * cols, cols)]
 
     def head_to(zz, cc, xx):
         return remote(
@@ -159,13 +154,6 @@
 
         lax.fori_loop(0, CHUNKS, one, 0)
 
-    def pass_far_head(d):
-        def both(zz):
-            for cc in range(CS):
-                pass_head(zz, cc, 1)
-
-        sides(d, both)
-
     def send_own(k, carry):
         @pl.when(z < ZS - 1)
         def _():
@@ -181,94 +169,55 @@
 
     lax.fori_loop(0, CHUNKS, send_own, 0)
     local = [pltpu.make_async_copy(strip(z, c, xx), wts_of(me, xx), s_l.at[xx]) for xx in range(XS)]
-    local.append(pltpu.make_async_copy(hid, tok.at[y, z, c], s_l.at[XS]))
+    whole = tok.at[pl.ds(pl.multiple_of((z * CS + c) * block, block), block), pl.ds(pl.multiple_of(y * feats, feats), feats)]
+    local.append(pltpu.make_async_copy(hid, whole, s_l.at[XS]))
     for copy in local:
         copy.start()
     for copy in local:
         copy.wait()
 
-    def first(k, carry):
-        @pl.when(k == CHUNKS // 2)
-        def _():
-            send_head(0)
-
-        pass_tokens(1, k)
+    for xx in range(XS):
+        send_head(xx)
+
+    def pass_all(d, carry):
+        for k in range(CHUNKS):
+            pass_tokens(d, k)
+
+        @pl.when(d == 1)
+        def _():
+            for xx in range(XS):
+                pass_head(z, 1 - c, xx)
+
+        def both(zz):
+            for cc in range(CS):
+                for xx in range(XS):
+                    pass_head(zz, cc, xx)
+
+        sides(d, both)
+
+        @pl.when(d == 1)
+        def _():
+            from_y(z)
+
+        @pl.when(d > 1)
+        def _():
+            sides(d - 1, from_y)
+
         return carry
 
-    def second(k, carry):
-        pass_tokens(2, k)
-        return carry
-
-    lax.fori_loop(0, CHUNKS, first, 0)
-    from_y(z)
-    lax.fori_loop(0, CHUNKS, second, 0)
-    send_head(1)
-    others(lambda zz, cc: pass_head(zz, cc, 0))
-    pass_head(z, 1 - c, 1)
-    sides(1, from_y)
-
-    def arrived(zz):
+    lax.fori_loop(1, ZS, pass_all, 0)
+    sides(ZS - 1, from_y)
+    for i in range(ZS * CS):
+        for xx in range(XS):
+            relay_from(i // CS, i % CS, xx).wait_recv()
+
+    def arrived(zz, carry):
         for f in range(2):
             for k in range(CHUNKS):
                 across_c(f, zz, k, piece(f, zz, 1 - c, k)).wait_recv()
-
-    def multiply(zz, cc, xx):
-        acc = jnp.dot(tok[0, zz, cc], wts[xx, pl.ds(0, feats)], preferred_element_type=jnp.float32)
-        acc += jnp.dot(tok[1, zz, cc], wts[xx, pl.ds(feats, feats)], preferred_element_type=jnp.float32)
-        top = jnp.max(acc.reshape(per, tokens_per, cols), axis=1)
-        start = pl.multiple_of((zz * CS + cc) * per, per)
-        pool[xx, pl.ds(start, per), :] = jnp.log1p(jnp.maximum(top, 0.0))
-
-    def step(j, carry):
-        @pl.when(j < STEPS)
-        def _():
-            for i in range(CHUNKS // STEPS):
-                pass_tokens(3, j * (CHUNKS // STEPS) + i)
-
-        @pl.when(j == 0)
-        def _():
-            for i in range(ZS * CS):
-                relay_from(i // CS, i % CS, 0).wait_recv()
-
-        @pl.when(j == STEPS - 1)
-        def _():
-            pass_far_head(1)
-            sides(2, from_y)
-
-        @pl.when(j == STEPS + 1)
-        def _():
-            pass_far_head(2)
-            sides(3, from_y)
-            pass_far_head(3)
-
-        d, s = (j + 1) // 2, (j + 1) % 2
-        zz = z + (1 - 2 * s) * d
-
-        @pl.when((zz >= 0) & (zz < ZS))
-        def _():
-            arrived(zz)
-
-            def core(cc, inner):
-                multiply(zz, cc, 0)
-                return inner
-
-            lax.fori_loop(0, CS, core, 0)
-
         return carry
 
-    lax.fori_loop(0, 2 * ZS - 1, step, 0)
-    for i in range(ZS * CS):
-        relay_from(i // CS, i % CS, 1).wait_recv()
-
-    def rest(i, carry):
-        multiply(i // CS, i % CS, 1)
-        return carry
-
-    lax.fori_loop(0, ZS * CS, rest, 0)
-
-    give[...] = pool[1 - x].astype(jnp.bfloat16)
-    last = remote(give, take, s_f, r_f, x_dev)
-    last.start()
+    lax.fori_loop(0, ZS, arrived, 0)
 
     def sent(zz, carry):
         for k in range(CHUNKS):
@@ -295,19 +244,6 @@
             head_to(zz, cc, xx).wait_send()
 
     others(head_sent)
-    last.wait()
-
-    mine = pool[x].astype(jnp.bfloat16).astype(jnp.float32)
-    theirs = take[...].astype(jnp.float32)
-    even = jnp.where(x == 0, mine, theirs)
-    odd = jnp.where(x == 0, theirs, mine)
-    span = CS * per
-    parts = []
-    for zz in range(ZS):
-        parts += [even[zz * span:(zz + 1) * span], odd[zz * span:(zz + 1) * span]]
-    full = jnp.concatenate(parts, axis=0)
-    peak = jnp.max(full, axis=0, keepdims=True)
-    out[...] = jnp.transpose(full / (1.0 + peak)).astype(jnp.bfloat16)
 
 
 def masked(hidden, lengths):
@@ -319,39 +255,41 @@
 
 def fused(hidden, head_weight, lengths):
     passages = lengths.shape[0]
-    tokens = hidden.shape[0]
-    feats = hidden.shape[1]
-    feat_rows = head_weight.shape[0]
-    cols = head_weight.shape[1] // (ZS * XS * CS)
-    rows = ZS * CS * passages
+    tokens, feats = hidden.shape
+    tokens_per = tokens // passages
+    owners = ZS * XS * CS
+    cols = head_weight.shape[1] // owners
     dma = pltpu.SemaphoreType.DMA
-    return pl.pallas_call(
-        functools.partial(kernel, tokens // passages),
-        out_shape=jax.ShapeDtypeStruct((cols, XS * rows), jnp.bfloat16),
+    gathered, weights = pl.pallas_call(
+        kernel,
+        out_shape=(
+            jax.ShapeDtypeStruct((ZS * CS * tokens, 2 * feats), jnp.bfloat16),
+            jax.ShapeDtypeStruct((2 * feats, XS * cols), jnp.bfloat16),
+        ),
         in_specs=[pl.BlockSpec(memory_space=pl.ANY)] * 2,
-        out_specs=pl.BlockSpec(memory_space=pltpu.VMEM),
+        out_specs=[pl.BlockSpec(memory_space=pl.ANY)] * 2,
         scratch_shapes=[
-            pltpu.VMEM((2, ZS, CS, tokens, feats), jnp.bfloat16),
-            pltpu.VMEM((XS, 2 * feats, cols), jnp.bfloat16),
-            pltpu.VMEM((XS, rows, cols), jnp.float32),
-            pltpu.VMEM((rows, cols), jnp.bfloat16),
-            pltpu.VMEM((rows, cols), jnp.bfloat16),
             dma((ZS, CHUNKS)), dma((ZS, CHUNKS)), dma((ZS, CHUNKS)),
             dma((ZS, CHUNKS)), dma((ZS, CHUNKS)),
             dma((2, ZS, CHUNKS)), dma((2, ZS, CHUNKS)),
             dma((ZS * CS, XS)), dma((ZS * CS, XS)),
             dma((ZS * CS, XS)), dma((ZS * CS, XS)),
-            dma, dma, dma((XS + 1,)),
+            dma((XS + 1,)),
         ],
-        compiler_params=pltpu.CompilerParams(
-            collective_id=0, has_side_effects=True, vmem_limit_bytes=HIGHEST_VMEM
-        ),
-        cost_estimate=pl.CostEstimate(
-            flops=2 * ZS * CS * tokens * 2 * feats * XS * cols,
-            bytes_accessed=2 * (tokens * feats + feat_rows * head_weight.shape[1]),
-            transcendentals=0,
-        ),
+        compiler_params=pltpu.CompilerParams(collective_id=0, has_side_effects=True),
     )(masked(hidden, lengths), head_weight)
+    logits = jnp.dot(gathered, weights, preferred_element_type=jnp.float32)
+    top = jnp.max(logits.reshape(ZS * CS * passages, tokens_per, XS * cols), axis=1)
+    pooled = jnp.log1p(jnp.maximum(top, 0.0)).astype(jnp.bfloat16)
+    x = (lax.axis_index("pass") // CS) % XS
+    swap = [(p, p + CS if (p // CS) % XS == 0 else p - CS) for p in range(owners)]
+    mine = lax.dynamic_slice_in_dim(pooled, x * cols, cols, 1)
+    theirs = lax.ppermute(lax.dynamic_slice_in_dim(pooled, (1 - x) * cols, cols, 1), "pass", swap)
+    even = jnp.where(x == 0, mine, theirs).reshape(ZS, CS * passages, cols)
+    odd = jnp.where(x == 0, theirs, mine).reshape(ZS, CS * passages, cols)
+    full = jnp.stack([even, odd], axis=1).reshape(owners * passages, cols).astype(jnp.float32)
+    peak = jnp.max(full, axis=0)
+    return jnp.transpose((full / (1.0 + peak)[None, :]).astype(jnp.bfloat16))
 
 
 def general(hidden, head_weight, lengths):

time: 288 us -> 323 us (1.12)
  the two profiles are of different devices: /device:TPU:8 before, /device:TPU:0 now
where the time goes in v4:
time: 323 us; the launch traced here: 322 us
  Pallas kernels  272 us (84%)
  matrix products  41.1 us (13%)
  other arithmetic  4.07 us (1%)
  waiting for transfers between devices  3.73 us (1%)
    pallas_call x1, Pallas kernels, fused(): pl.pallas_call(kernel, out_shape=(jax.ShapeDtypeStruct((ZS * CS * tokens,...  272 us
    dot_general x1, matrix products, fused(): logits = jnp.dot(gathered, weights, preferred_element_type=jnp.float32)  41.1 us
  transfers between devices with their start and end apart: 1, of which 1 were waited for; matrix products, arithmetic and copies ran while one was open for 0% of the time, Pallas kernels for 0%

profile of v4, /device:TPU:0, one launch (start us, length us, event | category | flops | bytes accessed | tf_op | source)
XLA Modules:
  0.0 322.5 jit_solution(17348699539020324216)
XLA Ops:
  0.0 0.7 iota_compare_fusion
  0.7 0.1 lt.36
  0.8 3.2 broadcast_select_fusion.hid
  4.0 272.0 %shard_map.37 = (bf16[4096,4096]{1,0:T(8,128)(2,1)}, bf16[4096,1024]{1,0:T(8,128)(2,1)}) custom-call(bf16[512,2048]{1,0:T(8,128)(2,1)} %broadcast_select_fusion.hid, bf16[256,8192]{1,0:T(8,128)(2,1)} %head.1), custom_call_target="tpu_custom_call" | custom-call | tf_op jit(solution)/shard_map/pallas_call | solution.py:263
  276.0 41.1 %bitcast_reduce_fusion = f32[64,1024]{1,0:T(8,128)S(1)} fusion(bf16[4096,4096]{1,0:T(8,128)(2,1)} %get-tuple-element.7, bf16[4096,1024]{1,0:T(8,128)(2,1)} %get-tuple-element.8), kind=kOutput, calls=%fused_computation | convolution fusion | flops 34363867136 | bytes 42205184 | tf_op jit(solution)/shard_map/dot_general | solution.py:281
  317.1 0.1 log-plus-one_convert_fusion
  317.2 0.6 collective-permute-start
  317.8 3.7 %collective-permute-done = bf16[64,512]{1,0:T(8,128)(2,1)S(1)} collective-permute-done((bf16[64,512]{1,0:T(8,128)(2,1)S(1)}, bf16[64,512]{1,0:T(8,128)(2,1)S(1)}, u32[]{:S(2)}, u32[]{:S(2)}) %collective-permute-start) | collective-permute-done | bytes 65568 | tf_op jit(solution)/shard_map/ppermute | solution.py:287
  321.7 0.8 copy.5
  (6 shorter events, 0.1 us)
Async XLA Ops:
  317.2 4.3 %collective-permute-start = (bf16[64,512]{1,0:T(8,128)(2,1)S(1)}, bf16[64,512]{1,0:T(8,128)(2,1)S(1)}, u32[]{:S(2)}, u32[]{:S(2)}) collective-permute-start(bf16[64,512]{1,0:T(8,128)(2,1)S(1)} %constant_dynamic-slice_fusion), channel_id=1, source_target_pairs={{0,2},{1,3},{2,0},{3,1},{4,6},{5,7},{6,4},{7,5},{8,10},{9,11},{10,... | collective-permute-start | bytes 196616 | tf_op jit(solution)/shard_map/ppermute | solution.py:287

commit v5 on v3

--- a/solution.py
+++ b/solution.py
@@ -10,7 +10,6 @@
 MESH = pl.DeviceIdType.MESH
 ZS, XS, CS = 4, 2, 2
 CHUNKS = 4
-STEPS = 4
 HIGHEST_VMEM = 58 * 1024 * 1024
 
 
@@ -85,6 +84,9 @@
     def wts_of(p, xx):
         return wts.at[xx, pl.ds(pl.multiple_of(p * feat_rows, feat_rows), feat_rows)]
 
+    def both_of(p):
+        return wts.at[:, pl.ds(pl.multiple_of(p * feat_rows, feat_rows), feat_rows)]
+
     def head_to(zz, cc, xx):
         return remote(
             strip(zz, cc, xx), wts_of(me, xx),
@@ -95,21 +97,18 @@
         ref = wts_of(at(zz, x, cc), xx)
         return remote(ref, ref, s_h.at[zz * CS + cc, xx], r_h.at[zz * CS + cc, xx], x_dev)
 
-    def relay(zz, cc, xx):
-        ref = wts_of(at(zz, x, cc), xx)
-        return remote(ref, ref, s_x.at[zz * CS + cc, xx], r_x.at[zz * CS + cc, xx], x_dev)
-
-    def relay_from(zz, cc, xx):
-        ref = wts_of(at(zz, 1 - x, cc), xx)
-        return remote(ref, ref, s_x.at[zz * CS + cc, xx], r_x.at[zz * CS + cc, xx], x_dev)
-
-    def send_head(xx):
-        others(lambda zz, cc: head_to(zz, cc, xx).start())
-        relay(z, c, xx).start()
-
-    def pass_head(zz, cc, xx):
-        head_from(zz, cc, xx).wait_recv()
-        relay(zz, cc, xx).start()
+    def relay(zz, cc):
+        ref = both_of(at(zz, x, cc))
+        return remote(ref, ref, s_x.at[zz * CS + cc], r_x.at[zz * CS + cc], x_dev)
+
+    def send_head(zz, cc):
+        for xx in range(XS):
+            head_to(zz, cc, xx).start()
+
+    def pass_head(zz, cc):
+        for xx in range(XS):
+            head_from(zz, cc, xx).wait_recv()
+        relay(zz, cc).start()
 
     def sides(d, do):
         def side(s, inner):
@@ -159,12 +158,18 @@
 
         lax.fori_loop(0, CHUNKS, one, 0)
 
-    def pass_far_head(d):
+    def near_head(d):
         def both(zz):
             for cc in range(CS):
-                pass_head(zz, cc, 1)
+                pass_head(zz, cc)
 
         sides(d, both)
+
+    local = [pltpu.make_async_copy(strip(z, c, xx), wts_of(me, xx), s_l.at[xx]) for xx in range(XS)]
+    local.append(pltpu.make_async_copy(hid, tok.at[y, z, c], s_l.at[XS]))
+    send_head(z, 1 - c)
+    for copy in local:
+        copy.start()
 
     def send_own(k, carry):
         @pl.when(z < ZS - 1)
@@ -177,94 +182,83 @@
 
         across_y(z, k, own_piece(k)).start()
         across_c(y, z, k, own_piece(k)).start()
+
+        for i in range(1, ZS):
+            @pl.when(k == i * CHUNKS // ZS - 1)
+            def _():
+                for cc in range(CS):
+                    send_head(lax.rem(z + i, ZS), cc)
+
         return carry
 
     lax.fori_loop(0, CHUNKS, send_own, 0)
-    local = [pltpu.make_async_copy(strip(z, c, xx), wts_of(me, xx), s_l.at[xx]) for xx in range(XS)]
-    local.append(pltpu.make_async_copy(hid, tok.at[y, z, c], s_l.at[XS]))
-    for copy in local:
-        copy.start()
     for copy in local:
         copy.wait()
-
-    def first(k, carry):
-        @pl.when(k == CHUNKS // 2)
-        def _():
-            send_head(0)
-
-        pass_tokens(1, k)
-        return carry
-
-    def second(k, carry):
-        pass_tokens(2, k)
-        return carry
-
-    lax.fori_loop(0, CHUNKS, first, 0)
-    from_y(z)
-    lax.fori_loop(0, CHUNKS, second, 0)
-    send_head(1)
-    others(lambda zz, cc: pass_head(zz, cc, 0))
-    pass_head(z, 1 - c, 1)
-    sides(1, from_y)
+    relay(z, c).start()
 
     def arrived(zz):
         for f in range(2):
             for k in range(CHUNKS):
                 across_c(f, zz, k, piece(f, zz, 1 - c, k)).wait_recv()
 
-    def multiply(zz, cc, xx):
-        acc = jnp.dot(tok[0, zz, cc], wts[xx, pl.ds(0, feats)], preferred_element_type=jnp.float32)
-        acc += jnp.dot(tok[1, zz, cc], wts[xx, pl.ds(feats, feats)], preferred_element_type=jnp.float32)
-        top = jnp.max(acc.reshape(per, tokens_per, cols), axis=1)
-        start = pl.multiple_of((zz * CS + cc) * per, per)
-        pool[xx, pl.ds(start, per), :] = jnp.log1p(jnp.maximum(top, 0.0))
-
-    def step(j, carry):
-        @pl.when(j < STEPS)
-        def _():
-            for i in range(CHUNKS // STEPS):
-                pass_tokens(3, j * (CHUNKS // STEPS) + i)
-
-        @pl.when(j == 0)
+    def multiply(zz, cc):
+        def half(xx, carry):
+            acc = jnp.dot(tok[0, zz, cc], wts[xx, pl.ds(0, feats)], preferred_element_type=jnp.float32)
+            acc += jnp.dot(tok[1, zz, cc], wts[xx, pl.ds(feats, feats)], preferred_element_type=jnp.float32)
+            top = jnp.max(acc.reshape(per, tokens_per, cols), axis=1)
+            first = pl.multiple_of((zz * CS + cc) * per, per)
+            pool[xx, pl.ds(first, per), :] = jnp.log1p(jnp.maximum(top, 0.0))
+            return carry
+
+        lax.fori_loop(0, XS, half, 0)
+
+    hops = (ZS - 1) * CHUNKS
+
+    def event(e, carry):
+        @pl.when(e < hops)
+        def _():
+            pass_tokens(1 + e // CHUNKS, lax.rem(e, CHUNKS))
+
+        @pl.when(e == 0)
+        def _():
+            pass_head(z, 1 - c)
+
+        for d in range(1, ZS):
+            @pl.when(e == d * CHUNKS // ZS)
+            def _():
+                near_head(d)
+
+        @pl.when(e == CHUNKS)
+        def _():
+            from_y(z)
+
+        @pl.when(e == hops - 6)
         def _():
             for i in range(ZS * CS):
-                relay_from(i // CS, i % CS, 0).wait_recv()
-
-        @pl.when(j == STEPS - 1)
-        def _():
-            pass_far_head(1)
-            sides(2, from_y)
-
-        @pl.when(j == STEPS + 1)
-        def _():
-            pass_far_head(2)
-            sides(3, from_y)
-            pass_far_head(3)
-
-        d, s = (j + 1) // 2, (j + 1) % 2
+                relay(i // CS, i % CS).wait_recv()
+
+        j = e - (hops - 5)
+        d, s = (j + 1) // 2, lax.rem(j + 1, 2)
         zz = z + (1 - 2 * s) * d
 
-        @pl.when((zz >= 0) & (zz < ZS))
+        for i in range(1, ZS):
+            @pl.when(j == 2 * i - 1)
+            def _():
+                sides(i, from_y)
+
+        @pl.when((j >= 0) & (zz >= 0) & (zz < ZS))
         def _():
             arrived(zz)
 
             def core(cc, inner):
-                multiply(zz, cc, 0)
+                multiply(zz, cc)
                 return inner
 
             lax.fori_loop(0, CS, core, 0)
 
         return carry
 
-    lax.fori_loop(0, 2 * ZS - 1, step, 0)
-    for i in range(ZS * CS):
-        relay_from(i // CS, i % CS, 1).wait_recv()
-
-    def rest(i, carry):
-        multiply(i // CS, i % CS, 1)
-        return carry
-
-    lax.fori_loop(0, ZS * CS, rest, 0)
+    lax.fori_loop(0, hops + 2, event, 0)
 
     give[...] = pool[1 - x].astype(jnp.bfloat16)
     last = remote(give, take, s_f, r_f, x_dev)
@@ -284,8 +278,7 @@
             for f in range(2):
                 across_c(f, zz, k, own_piece(k)).wait_send()
         for cc in range(CS):
-            for xx in range(XS):
-                relay(zz, cc, xx).wait_send()
+            relay(zz, cc).wait_send()
         return carry
 
     lax.fori_loop(0, ZS, sent, 0)
@@ -340,7 +333,7 @@
             dma((ZS, CHUNKS)), dma((ZS, CHUNKS)),
             dma((2, ZS, CHUNKS)), dma((2, ZS, CHUNKS)),
             dma((ZS * CS, XS)), dma((ZS * CS, XS)),
-            dma((ZS * CS, XS)), dma((ZS * CS, XS)),
+            dma((ZS * CS,)), dma((ZS * CS,)),
             dma, dma, dma((XS + 1,)),
         ],
         compiler_params=pltpu.CompilerParams(

time: 288 us -> 250 us (0.87)
  the two profiles are of different devices: /device:TPU:8 before, /device:TPU:0 now
where the time goes in v5:
time: 250 us
  Pallas kernels  244 us (98%)
  other arithmetic  3.88 us (2%)
    pallas_call x1, Pallas kernels, fused(): pl.pallas_call(functools.partial(kernel, tokens // passages), out_shape=j...  244 us

profile of v5, /device:TPU:0, one launch (start us, length us, event | category | flops | bytes accessed | tf_op | source)
XLA Modules:
  0.0 249.5 jit_solution(428732397238006731)
XLA Ops:
  0.0 0.7 iota_compare_fusion
  0.7 0.1 lt.23
  0.8 3.2 %broadcast_select_fusion.hid = bf16[512,2048]{1,0:T(8,128)(2,1)} fusion(bf16[512,2048]{1,0:T(8,128)(2,1)} %param.3, pred[512]{0:T(512)(128)(4,1)S(1)} %lt.23), kind=kLoop, calls=%fused_computation | loop fusion | flops 1048576 | bytes 4194816 | tf_op jit(solution)/shard_map/jit(_where)/select_n | solution.py:310
  4.0 244.0 %shard_map.37 = bf16[512,128]{1,0:T(8,128)(2,1)} custom-call(bf16[512,2048]{1,0:T(8,128)(2,1)} %broadcast_select_fusion.hid, bf16[256,8192]{1,0:T(8,128)(2,1)} %head.1), custom_call_target="tpu_custom_call" | custom-call | flops 34359738368 | bytes 6291456 | tf_op jit(solution)/shard_map/pallas_call | solution.py:321
  247.9 1.6 copy.5

commit v6 on v5

--- a/solution.py
+++ b/solution.py
@@ -14,9 +14,9 @@
 
 
 def kernel(
-    tokens_per, hid, head, out,
+    tokens_per, lens, hid, head, out,
     tok, wts, pool, give, take,
-    s_up, s_dn, r_z, s_y, r_y, s_c, r_c, s_h, r_h, s_x, r_x, s_f, r_f, s_l,
+    s_up, s_dn, r_z, s_y, r_y, s_c, r_c, s_h, r_h, s_x, r_x, s_f, r_f, s_l, s_t,
 ):
     y = lax.axis_index("term")
     me = lax.axis_index("pass")
@@ -43,6 +43,15 @@
                 do(zz, cc)
         do(z, 1 - c)
 
+    loads = [
+        pltpu.make_async_copy(
+            hid.at[pl.ds(k * rows, rows)], tok.at[y, z, c, pl.ds(k * rows, rows)], s_t.at[k]
+        )
+        for k in range(CHUNKS)
+    ]
+    for load in loads:
+        load.start()
+
     barrier = pltpu.get_barrier_semaphore()
 
     def hello(dev):
@@ -63,7 +72,7 @@
         return tok.at[f, zz, cc, pl.ds(k * rows, rows)]
 
     def own_piece(k):
-        return hid.at[pl.ds(k * rows, rows)]
+        return piece(y, z, c, k)
 
     def up(zz, k, src):
         return remote(src, piece(y, zz, c, k), s_up.at[zz, k], r_z.at[zz, k], up_dev)
@@ -166,10 +175,17 @@
         sides(d, both)
 
     local = [pltpu.make_async_copy(strip(z, c, xx), wts_of(me, xx), s_l.at[xx]) for xx in range(XS)]
-    local.append(pltpu.make_async_copy(hid, tok.at[y, z, c], s_l.at[XS]))
     send_head(z, 1 - c)
     for copy in local:
         copy.start()
+
+    slots = lax.broadcasted_iota(jnp.int32, (tokens_per, feats), 0)
+    for k in range(CHUNKS):
+        loads[k].wait()
+        for i in range(k * rows // tokens_per, (k + 1) * rows // tokens_per):
+            own = (y, z, c, pl.ds(i * tokens_per, tokens_per))
+            kept = jnp.where(slots < lens[i], tok[own].astype(jnp.float32), 0.0)
+            tok[own] = kept.astype(jnp.bfloat16)
 
     def send_own(k, carry):
         @pl.when(z < ZS - 1)
@@ -196,21 +212,30 @@
         copy.wait()
     relay(z, c).start()
 
-    def arrived(zz):
+    def arrived(zz, h):
         for f in range(2):
-            for k in range(CHUNKS):
-                across_c(f, zz, k, piece(f, zz, 1 - c, k)).wait_recv()
-
-    def multiply(zz, cc):
-        def half(xx, carry):
-            acc = jnp.dot(tok[0, zz, cc], wts[xx, pl.ds(0, feats)], preferred_element_type=jnp.float32)
-            acc += jnp.dot(tok[1, zz, cc], wts[xx, pl.ds(feats, feats)], preferred_element_type=jnp.float32)
-            top = jnp.max(acc.reshape(per, tokens_per, cols), axis=1)
+            for k in range(CHUNKS // 2):
+                at_k = h * (CHUNKS // 2) + k
+                across_c(f, zz, at_k, piece(f, zz, 1 - c, at_k)).wait_recv()
+
+    def multiply(zz, h):
+        tall = block // 2
+
+        def part(i, carry):
+            cc, xx = i // XS, lax.rem(i, XS)
+            span = pl.ds(pl.multiple_of(h * tall, tall), tall)
+            acc = jnp.dot(tok[0, zz, cc, span], wts[xx, pl.ds(0, feats)], preferred_element_type=jnp.float32)
+            acc += jnp.dot(tok[1, zz, cc, span], wts[xx, pl.ds(feats, feats)], preferred_element_type=jnp.float32)
+            top = jnp.max(acc.reshape(per // 2, tokens_per, cols), axis=1)
+            top = jnp.log1p(jnp.maximum(top, 0.0))
+            both = jnp.concatenate([top, top], axis=0)
+            place = lax.broadcasted_iota(jnp.int32, both.shape, 0) // (per // 2)
             first = pl.multiple_of((zz * CS + cc) * per, per)
-            pool[xx, pl.ds(first, per), :] = jnp.log1p(jnp.maximum(top, 0.0))
+            old = jnp.where(h == 0, 0.0, pool[xx, pl.ds(first, per), :])
+            pool[xx, pl.ds(first, per), :] = jnp.where(place == h, both, old)
             return carry
 
-        lax.fori_loop(0, XS, half, 0)
+        lax.fori_loop(0, CS * XS, part, 0)
 
     hops = (ZS - 1) * CHUNKS
 
@@ -232,33 +257,43 @@
         def _():
             from_y(z)
 
-        @pl.when(e == hops - 6)
+        @pl.when(e == lead - CHUNKS // 4)
         def _():
             for i in range(ZS * CS):
                 relay(i // CS, i % CS).wait_recv()
 
-        j = e - (hops - 5)
-        d, s = (j + 1) // 2, lax.rem(j + 1, 2)
-        zz = z + (1 - 2 * s) * d
-
-        for i in range(1, ZS):
-            @pl.when(j == 2 * i - 1)
-            def _():
-                sides(i, from_y)
-
-        @pl.when((j >= 0) & (zz >= 0) & (zz < ZS))
-        def _():
-            arrived(zz)
-
-            def core(cc, inner):
-                multiply(zz, cc)
+        j = (e - lead) // (CHUNKS // 4)
+        low = z < ZS // 2
+        near = jnp.where(z == 0, 1, z - 1)
+        far = jnp.where(z == ZS - 1, -1, z + 1)
+        zz = jnp.where(j == 0, z, jnp.where(j == 1, near, jnp.where(j == 2, far, jnp.where(
+            j == 3, jnp.where(low, z + 2, z - 2), jnp.where(low, z + 3, z - 3)))))
+        there = (j >= 0) & (j < 6) & (lax.rem(e - lead, CHUNKS // 4) == 0) & (zz >= 0) & (zz < ZS)
+        there = there & ((j != 2) | (z > 0))
+        begin = jnp.where(j == 5, 1, 0)
+        end = jnp.where(j == 4, 1, 2)
+
+        @pl.when(there)
+        def _():
+            def halves(h, inner):
+                @pl.when(j > 0)
+                def _():
+                    for k in range(CHUNKS // 2):
+                        at_k = h * (CHUNKS // 2) + k
+                        src = piece(1 - y, zz, c, at_k)
+                        across_y(zz, at_k, src).wait_recv()
+                        across_c(1 - y, zz, at_k, src).start()
+
+                arrived(zz, h)
+                multiply(zz, h)
                 return inner
 
-            lax.fori_loop(0, CS, core, 0)
+            lax.fori_loop(begin, end, halves, 0)
 
         return carry
 
-    lax.fori_loop(0, hops + 2, event, 0)
+    lead = hops - 5 * CHUNKS // 4
+    lax.fori_loop(0, hops + CHUNKS // 4, event, 0)
 
     give[...] = pool[1 - x].astype(jnp.bfloat16)
     last = remote(give, take, s_f, r_f, x_dev)
@@ -321,7 +356,7 @@
     return pl.pallas_call(
         functools.partial(kernel, tokens // passages),
         out_shape=jax.ShapeDtypeStruct((cols, XS * rows), jnp.bfloat16),
-        in_specs=[pl.BlockSpec(memory_space=pl.ANY)] * 2,
+        in_specs=[pl.BlockSpec(memory_space=pltpu.SMEM)] + [pl.BlockSpec(memory_space=pl.ANY)] * 2,
         out_specs=pl.BlockSpec(memory_space=pltpu.VMEM),
         scratch_shapes=[
             pltpu.VMEM((2, ZS, CS, tokens, feats), jnp.bfloat16),
@@ -334,7 +369,7 @@
             dma((2, ZS, CHUNKS)), dma((2, ZS, CHUNKS)),
             dma((ZS * CS, XS)), dma((ZS * CS, XS)),
             dma((ZS * CS,)), dma((ZS * CS,)),
-            dma, dma, dma((XS + 1,)),
+            dma, dma, dma((XS,)), dma((CHUNKS,)),
         ],
         compiler_params=pltpu.CompilerParams(
             collective_id=0, has_side_effects=True, vmem_limit_bytes=HIGHEST_VMEM
@@ -344,7 +379,7 @@
             bytes_accessed=2 * (tokens * feats + feat_rows * head_weight.shape[1]),
             transcendentals=0,
         ),
-    )(masked(hidden, lengths), head_weight)
+    )(lengths, hidden, head_weight)
 
 
 def general(hidden, head_weight, lengths):

time: 250 us -> 251 us (level)
  the two profiles are of different devices: /device:TPU:0 before, /device:TPU:13 now
where the time goes in v6:
time: 251 us
  Pallas kernels  249 us (99%)
    pallas_call x1, Pallas kernels, fused(): pl.pallas_call(functools.partial(kernel, tokens // passages), out_shape=j...  249 us

profile of v6, /device:TPU:13, one launch (start us, length us, event | category | flops | bytes accessed | tf_op | source)
XLA Modules:
  0.0 250.8 jit_solution(12955553854523626563)
XLA Ops:
  0.0 249.2 %shard_map.37 = bf16[512,128]{1,0:T(8,128)(2,1)} custom-call(s32[8]{0:T(128)} %lens.1, bf16[512,2048]{1,0:T(8,128)(2,1)} %hid.1, bf16[256,8192]{1,0:T(8,128)(2,1)} %head.1), custom_call_target="tpu_custom_call" | custom-call | flops 34359738368 | bytes 6291456 | tf_op jit(solution)/shard_map/pallas_call | solution.py:356
  249.2 1.6 copy.5

commit v7 on v6

--- a/solution.py
+++ b/solution.py
@@ -257,18 +257,19 @@
         def _():
             from_y(z)
 
-        @pl.when(e == lead - CHUNKS // 4)
+        @pl.when(e == lead)
         def _():
             for i in range(ZS * CS):
                 relay(i // CS, i % CS).wait_recv()
 
-        j = (e - lead) // (CHUNKS // 4)
+        j = e - lead
+        j = jnp.where(j >= 5, j - 2, jnp.where(j >= 3, -1, j))
         low = z < ZS // 2
         near = jnp.where(z == 0, 1, z - 1)
         far = jnp.where(z == ZS - 1, -1, z + 1)
         zz = jnp.where(j == 0, z, jnp.where(j == 1, near, jnp.where(j == 2, far, jnp.where(
             j == 3, jnp.where(low, z + 2, z - 2), jnp.where(low, z + 3, z - 3)))))
-        there = (j >= 0) & (j < 6) & (lax.rem(e - lead, CHUNKS // 4) == 0) & (zz >= 0) & (zz < ZS)
+        there = (j >= 0) & (j < 6) & (zz >= 0) & (zz < ZS)
         there = there & ((j != 2) | (z > 0))
         begin = jnp.where(j == 5, 1, 0)
         end = jnp.where(j == 4, 1, 2)
@@ -292,8 +293,8 @@
 
         return carry
 
-    lead = hops - 5 * CHUNKS // 4
-    lax.fori_loop(0, hops + CHUNKS // 4, event, 0)
+    lead = hops - 7
+    lax.fori_loop(0, hops + 1, event, 0)
 
     give[...] = pool[1 - x].astype(jnp.bfloat16)
     last = remote(give, take, s_f, r_f, x_dev)

time: 251 us -> 265 us (1.056)
  the two profiles are of different devices: /device:TPU:13 before, /device:TPU:0 now
where the time goes in v7:
time: 265 us; the launch traced here: 264 us
  Pallas kernels  263 us (99%)
    pallas_call x1, Pallas kernels, fused(): pl.pallas_call(functools.partial(kernel, tokens // passages), out_shape=j...  263 us

profile of v7, /device:TPU:0, one launch (start us, length us, event | category | flops | bytes accessed | tf_op | source)
XLA Modules:
  0.0 264.4 jit_solution(5635929824581818278)
XLA Ops:
  0.0 262.8 %shard_map.37 = bf16[512,128]{1,0:T(8,128)(2,1)} custom-call(s32[8]{0:T(128)} %lens.1, bf16[512,2048]{1,0:T(8,128)(2,1)} %hid.1, bf16[256,8192]{1,0:T(8,128)(2,1)} %head.1), custom_call_target="tpu_custom_call" | custom-call | flops 34359738368 | bytes 6291456 | tf_op jit(solution)/shard_map/pallas_call | solution.py:357
  262.8 1.6 copy.5

commit v8 on v6

--- a/solution.py
+++ b/solution.py
@@ -202,8 +202,11 @@
         for i in range(1, ZS):
             @pl.when(k == i * CHUNKS // ZS - 1)
             def _():
-                for cc in range(CS):
-                    send_head(lax.rem(z + i, ZS), cc)
+                def strips(zz):
+                    for cc in range(CS):
+                        send_head(zz, cc)
+
+                sides(i, strips)
 
         return carry
 
@@ -257,7 +260,7 @@
         def _():
             from_y(z)
 
-        @pl.when(e == lead - CHUNKS // 4)
+        @pl.when(e == lead)
         def _():
             for i in range(ZS * CS):
                 relay(i // CS, i % CS).wait_recv()

time: 251 us -> 249 us (level)
  the two profiles are of different devices: /device:TPU:13 before, /device:TPU:12 now
where the time goes in v8:
time: 249 us
  Pallas kernels  247 us (99%)
    pallas_call x1, Pallas kernels, fused(): pl.pallas_call(functools.partial(kernel, tokens // passages), out_shape=j...  247 us

profile of v8, /device:TPU:12, one launch (start us, length us, event | category | flops | bytes accessed | tf_op | source)
XLA Modules:
  0.0 248.9 jit_solution(16751211985155238932)
XLA Ops:
  0.0 247.3 %shard_map.37 = bf16[512,128]{1,0:T(8,128)(2,1)} custom-call(s32[8]{0:T(128)} %lens.1, bf16[512,2048]{1,0:T(8,128)(2,1)} %hid.1, bf16[256,8192]{1,0:T(8,128)(2,1)} %head.1), custom_call_target="tpu_custom_call" | custom-call | flops 34359738368 | bytes 6291456 | tf_op jit(solution)/shard_map/pallas_call | solution.py:359
  247.3 1.6 copy.5

commit v9 on v8

--- a/solution.py
+++ b/solution.py
@@ -215,30 +215,22 @@
         copy.wait()
     relay(z, c).start()
 
-    def arrived(zz, h):
+    def arrived(zz):
         for f in range(2):
-            for k in range(CHUNKS // 2):
-                at_k = h * (CHUNKS // 2) + k
-                across_c(f, zz, at_k, piece(f, zz, 1 - c, at_k)).wait_recv()
-
-    def multiply(zz, h):
-        tall = block // 2
-
-        def part(i, carry):
-            cc, xx = i // XS, lax.rem(i, XS)
-            span = pl.ds(pl.multiple_of(h * tall, tall), tall)
-            acc = jnp.dot(tok[0, zz, cc, span], wts[xx, pl.ds(0, feats)], preferred_element_type=jnp.float32)
-            acc += jnp.dot(tok[1, zz, cc, span], wts[xx, pl.ds(feats, feats)], preferred_element_type=jnp.float32)
-            top = jnp.max(acc.reshape(per // 2, tokens_per, cols), axis=1)
-            top = jnp.log1p(jnp.maximum(top, 0.0))
-            both = jnp.concatenate([top, top], axis=0)
-            place = lax.broadcasted_iota(jnp.int32, both.shape, 0) // (per // 2)
-            first = pl.multiple_of((zz * CS + cc) * per, per)
-            old = jnp.where(h == 0, 0.0, pool[xx, pl.ds(first, per), :])
-            pool[xx, pl.ds(first, per), :] = jnp.where(place == h, both, old)
+            for k in range(CHUNKS):
+                across_c(f, zz, k, piece(f, zz, 1 - c, k)).wait_recv()
+
+    def multiply(zz):
+        def half(xx, carry):
+            first, second = (tok[f, zz].reshape(CS * block, feats) for f in range(2))
+            acc = jnp.dot(first, wts[xx, pl.ds(0, feats)], preferred_element_type=jnp.float32)
+            acc += jnp.dot(second, wts[xx, pl.ds(feats, feats)], preferred_element_type=jnp.float32)
+            top = jnp.max(acc.reshape(CS * per, tokens_per, cols), axis=1)
+            place = pl.ds(pl.multiple_of(zz * CS * per, CS * per), CS * per)
+            pool[xx, place, :] = jnp.log1p(jnp.maximum(top, 0.0))
             return carry
 
-        lax.fori_loop(0, CS * XS, part, 0)
+        lax.fori_loop(0, XS, half, 0)
 
     hops = (ZS - 1) * CHUNKS
 
@@ -265,33 +257,21 @@
             for i in range(ZS * CS):
                 relay(i // CS, i % CS).wait_recv()
 
-        j = (e - lead) // (CHUNKS // 4)
+        j = e - lead
         low = z < ZS // 2
         near = jnp.where(z == 0, 1, z - 1)
-        far = jnp.where(z == ZS - 1, -1, z + 1)
+        far = jnp.where((z == 0) | (z == ZS - 1), -1, z + 1)
         zz = jnp.where(j == 0, z, jnp.where(j == 1, near, jnp.where(j == 2, far, jnp.where(
             j == 3, jnp.where(low, z + 2, z - 2), jnp.where(low, z + 3, z - 3)))))
-        there = (j >= 0) & (j < 6) & (lax.rem(e - lead, CHUNKS // 4) == 0) & (zz >= 0) & (zz < ZS)
-        there = there & ((j != 2) | (z > 0))
-        begin = jnp.where(j == 5, 1, 0)
-        end = jnp.where(j == 4, 1, 2)
-
-        @pl.when(there)
-        def _():
-            def halves(h, inner):
-                @pl.when(j > 0)
-                def _():
-                    for k in range(CHUNKS // 2):
-                        at_k = h * (CHUNKS // 2) + k
-                        src = piece(1 - y, zz, c, at_k)
-                        across_y(zz, at_k, src).wait_recv()
-                        across_c(1 - y, zz, at_k, src).start()
-
-                arrived(zz, h)
-                multiply(zz, h)
-                return inner
-
-            lax.fori_loop(begin, end, halves, 0)
+
+        @pl.when((j >= 0) & (j != 4) & (zz >= 0) & (zz < ZS))
+        def _():
+            @pl.when(j > 0)
+            def _():
+                from_y(zz)
+
+            arrived(zz)
+            multiply(zz)
 
         return carry
 

time: 249 us -> 244 us (0.980)
  the two profiles are of different devices: /device:TPU:12 before, /device:TPU:0 now
where the time goes in v9:
time: 244 us
  Pallas kernels  243 us (100%)
    pallas_call x1, Pallas kernels, fused(): pl.pallas_call(functools.partial(kernel, tokens // passages), out_shape=j...  243 us

profile of v9, /device:TPU:0, one launch (start us, length us, event | category | flops | bytes accessed | tf_op | source)
XLA Modules:
  0.0 244.3 jit_solution(10941102283435766717)
XLA Ops:
  0.0 242.8 %shard_map.37 = bf16[512,128]{1,0:T(8,128)(2,1)} custom-call(s32[8]{0:T(128)} %lens.1, bf16[512,2048]{1,0:T(8,128)(2,1)} %hid.1, bf16[256,8192]{1,0:T(8,128)(2,1)} %head.1), custom_call_target="tpu_custom_call" | custom-call | flops 34359738368 | bytes 6291456 | tf_op jit(solution)/shard_map/pallas_call | solution.py:339
  242.8 1.6 copy.5

commit v10 on v9

--- a/solution.py
+++ b/solution.py
@@ -262,9 +262,9 @@
         near = jnp.where(z == 0, 1, z - 1)
         far = jnp.where((z == 0) | (z == ZS - 1), -1, z + 1)
         zz = jnp.where(j == 0, z, jnp.where(j == 1, near, jnp.where(j == 2, far, jnp.where(
-            j == 3, jnp.where(low, z + 2, z - 2), jnp.where(low, z + 3, z - 3)))))
-
-        @pl.when((j >= 0) & (j != 4) & (zz >= 0) & (zz < ZS))
+            j == 4, jnp.where(low, z + 2, z - 2), jnp.where(low, z + 3, z - 3)))))
+
+        @pl.when((j >= 0) & (j != 3) & (zz >= 0) & (zz < ZS))
         def _():
             @pl.when(j > 0)
             def _():

time: 244 us -> 245 us (level)
  no operation moved by 1% of the time
where the time goes in v10:
time: 245 us
  Pallas kernels  243 us (99%)
    pallas_call x1, Pallas kernels, fused(): pl.pallas_call(functools.partial(kernel, tokens // passages), out_shape=j...  243 us

profile of v10, /device:TPU:0, one launch (start us, length us, event | category | flops | bytes accessed | tf_op | source)
XLA Modules:
  0.0 244.5 jit_solution(4468041058425381851)
XLA Ops:
  0.0 242.9 %shard_map.37 = bf16[512,128]{1,0:T(8,128)(2,1)} custom-call(s32[8]{0:T(128)} %lens.1, bf16[512,2048]{1,0:T(8,128)(2,1)} %hid.1, bf16[256,8192]{1,0:T(8,128)(2,1)} %head.1), custom_call_target="tpu_custom_call" | custom-call | flops 34359738368 | bytes 6291456 | tf_op jit(solution)/shard_map/pallas_call | solution.py:339
  242.9 1.6 copy.5
